TPU v7x, 32 devices: a whole 2x2x4 slice. The times are simulated.
32 devices in a mesh: seq: 16 (over z, y, x), ch: 2 (over core).
Axes of the slice: x: 2, y: 2, z: 4, core: 2. Of those that a mesh axis runs over, the one named last changes fastest.
Arguments:
- gate_outer: bfloat16 [2048, 4096], P('seq', 'ch'), may hold values from -6 to 6
- gate_inner: bfloat16 [2048, 4096], P('seq', 'ch'), may hold values from -6 to 6
- values_in: bfloat16 [2048, 4096], P('seq', 'ch'), may hold values from -6 to 6
- filter_taps: bfloat16 [2048, 512], P('seq', 'ch'), may hold values from -2.5 to 2.5
- skip_gain: float32 [4096], P('ch'), may hold values from -4 to 4
Outputs:
- mixed_output: bfloat16 [2048, 4096], P('seq', 'ch')
All inputs are finite; a program needn't handle non-finite values.
Results may differ from a plain program's by a relative error of at most 0.0065.
Values may be sent and summed in bfloat16 or wider, within the bound.
A program may use at most 64 MiB of HBM per device.

v0:
```python
import math

import jax
import jax.numpy as jnp
from jax import lax
from jax.sharding import PartitionSpec as P

HIGHEST = lax.Precision.HIGHEST


def angle_table(first_index, second_index, modulus):
    product = first_index[:, None] * second_index[None, :] % modulus
    radians = product.astype(jnp.float32) * (2.0 * math.pi / modulus)
    return (jnp.cos(radians), jnp.sin(radians))


def contract(form, table, operand):
    return jnp.einsum(form, table, operand, precision=HIGHEST)


def complex_contract(form, cosine, sine, sign, real_part, imag_part):
    out_real = contract(form, cosine, real_part) - sign * contract(form, sine, imag_part)
    out_imag = contract(form, cosine, imag_part) + sign * contract(form, sine, real_part)
    return (out_real, out_imag)


def rotate(real_part, imag_part, cosine, sine):
    return (real_part * cosine - imag_part * sine, real_part * sine + imag_part * cosine)


def four_step(mixed_input, filter_taps):
    seq_count = lax.axis_size("seq")
    seq_index = lax.axis_index("seq")
    length_dev, width_dev = mixed_input.shape
    class_rows = length_dev // seq_count
    fft_size = 2 * length_dev * seq_count
    filter_local = lax.all_gather(filter_taps, "ch", axis=1, tiled=True)
    got_input, got_filter = (
        lax.all_to_all(mixed_input[None], "seq", split_axis=1, concat_axis=0, tiled=True),
        lax.all_to_all(filter_local[None], "seq", split_axis=1, concat_axis=0, tiled=True),
    )
    got_input = got_input.astype(jnp.float32)
    got_filter = got_filter.astype(jnp.float32)
    source = jnp.arange(seq_count, dtype=jnp.int32)
    pair_second = jnp.where(source == 0, seq_count, 2 * seq_count - source)
    cos_first, sin_first = angle_table(source, source, 2 * seq_count)
    at_zero = seq_index == 0
    cos_second, sin_second = angle_table(pair_second, source, 2 * seq_count)

    def send_parts(received):
        return jnp.stack(
            [
                contract("dp,prc->drc", cos_first, received),
                -contract("dp,prc->drc", sin_first, received),
                contract("dp,prc->drc", cos_second, received),
                -contract("dp,prc->drc", sin_second, received),
            ],
            axis=1,
        )

    sent_input, sent_filter = (
        lax.all_to_all(send_parts(got_input), "seq", split_axis=0, concat_axis=0, tiled=True),
        lax.all_to_all(send_parts(got_filter), "seq", split_axis=0, concat_axis=0, tiled=True),
    )

    def unpack(spectra):
        return (
            jnp.stack([spectra[:, 0], spectra[:, 2]], axis=0),
            jnp.stack([spectra[:, 1], spectra[:, 3]], axis=0),
        )

    my_pair = jnp.stack([seq_index, jnp.where(at_zero, seq_count, 2 * seq_count - seq_index)])
    positions = jnp.arange(length_dev, dtype=jnp.int32)
    cos_twist, sin_twist = angle_table(my_pair, positions, fft_size)
    cos_twist = cos_twist.reshape(2, seq_count, class_rows)
    sin_twist = sin_twist.reshape(2, seq_count, class_rows)
    cos_outer, sin_outer = angle_table(source, source, seq_count)
    inner_index = jnp.arange(class_rows, dtype=jnp.int32)
    cos_mid, sin_mid = angle_table(source, inner_index, length_dev)
    cos_inner, sin_inner = angle_table(inner_index, inner_index, class_rows)

    def finish(spec_real, spec_imag):
        spec_real, spec_imag = rotate(
            spec_real, spec_imag, cos_twist[:, :, :, None], -sin_twist[:, :, :, None]
        )
        spec_real, spec_imag = complex_contract(
            "aq,kqrc->karc", cos_outer, sin_outer, -1.0, spec_real, spec_imag
        )
        spec_real, spec_imag = rotate(
            spec_real, spec_imag, cos_mid[None, :, :, None], -sin_mid[None, :, :, None]
        )
        return complex_contract("br,karc->kabc", cos_inner, sin_inner, -1.0, spec_real, spec_imag)

    input_real, input_imag = finish(*unpack(sent_input))
    filter_real, filter_imag = finish(*unpack(sent_filter))
    repeat = width_dev // filter_real.shape[3]
    filter_real = jnp.tile(filter_real, (1, 1, 1, repeat))
    filter_imag = jnp.tile(filter_imag, (1, 1, 1, repeat))
    prod_real = input_real * filter_real - input_imag * filter_imag
    prod_imag = input_real * filter_imag + input_imag * filter_real
    prod_real, prod_imag = complex_contract(
        "br,kabc->karc", cos_inner, sin_inner, 1.0, prod_real, prod_imag
    )
    prod_real, prod_imag = rotate(
        prod_real, prod_imag, cos_mid[None, :, :, None], sin_mid[None, :, :, None]
    )
    prod_real, prod_imag = complex_contract(
        "aq,karc->kqrc", cos_outer, sin_outer, 1.0, prod_real, prod_imag
    )
    prod_real, prod_imag = rotate(
        prod_real, prod_imag, cos_twist[:, :, :, None], sin_twist[:, :, :, None]
    )
    cos_back, sin_back = angle_table(source, source, 2 * seq_count)
    parts_back = jnp.stack([prod_real[0], prod_imag[0], prod_real[1], prod_imag[1]], axis=1)
    partial_value = lax.all_to_all(parts_back, "seq", split_axis=0, concat_axis=0, tiled=True)
    cos_other, sin_other = angle_table(source, pair_second, 2 * seq_count)
    convolved = (
        contract("pd,drc->prc", cos_back, partial_value[:, 0])
        - contract("pd,drc->prc", sin_back, partial_value[:, 1])
        + contract("pd,drc->prc", cos_other, partial_value[:, 2])
        - contract("pd,drc->prc", sin_other, partial_value[:, 3])
    ) / fft_size
    return lax.all_to_all(convolved, "seq", split_axis=0, concat_axis=1, tiled=True).reshape(
        length_dev, width_dev
    )


def on_device(gate_outer, gate_inner, values_in, filter_taps, skip_gain):
    mixed_input = (gate_inner.astype(jnp.float32) * values_in.astype(jnp.float32)).astype(
        jnp.bfloat16
    )
    convolved = four_step(mixed_input, filter_taps)
    gated = gate_outer.astype(jnp.float32) * (
        convolved + skip_gain[None, :] * mixed_input.astype(jnp.float32)
    )
    return gated.astype(jnp.bfloat16)


def solution(mesh):
    return jax.shard_map(
        on_device,
        mesh=mesh,
        in_specs=(P("seq", "ch"), P("seq", "ch"), P("seq", "ch"), P("seq", "ch"), P("ch")),
        out_specs=P("seq", "ch"),
        check_vma=False,
    )
```

profile of v0, /device:TPU:0, one launch (start us, length us, event | category | flops | bytes accessed | tf_op | source)
XLA Modules:
  0.0 361.3 jit_solution(2569099726032763897)
XLA Ops:
  0.0 2.4 all_gather.3
  5.2 8.2 %all-to-all-start.2 = ((bf16[16,2,2048]{2,1,0:T(2,128)(2,1)}), bf16[16,2,2048]{2,1,0:T(2,128)(2,1)S(1)}, u32[]{:S(2)}, u32[]{:S(2)}) async-start(bf16[16,2,2048]{2,1,0:T(2,128)(2,1)} %reshape.185), calls=%async_computation.2 | async-start | bytes 262144 | tf_op jit(solution)/shard_map/all_to_all | solution.py:40
  15.6 3.7 %reduce.1 = bf16[128,2048]{1,0:T(8,128)(2,1)S(1)} reduce(bf16[128,1,2048]{2,1,0:T(2,128)(2,1)S(1)} %bitcast.232, bf16[]{:T(256)} %broadcast.514), dimensions={1}, to_apply=%bitcast.223.reduce_sub_computation | reduce | bytes 1048578
  21.2 6.3 %all-to-all-start = ((bf16[16,2,8192]{2,1,0:T(2,128)(2,1)}), bf16[16,2,8192]{2,1,0:T(2,128)(2,1)S(1)}, u32[]{:S(2)}, u32[]{:S(2)}) async-start(bf16[16,2,8192]{2,1,0:T(2,128)(2,1)} %reshape.183), calls=%async_computation | async-start | bytes 1048576 | tf_op jit(solution)/shard_map/all_to_all | solution.py:39
  29.2 1.6 copy.142
  30.8 11.6 %all-to-all-done = bf16[16,2,8192]{2,1,0:T(2,128)(2,1)S(1)} async-done(((bf16[16,2,8192]{2,1,0:T(2,128)(2,1)}), bf16[16,2,8192]{2,1,0:T(2,128)(2,1)S(1)}, u32[]{:S(2)}, u32[]{:S(2)}) %all-to-all-start) | async-done | bytes 524320 | tf_op jit(solution)/shard_map/all_to_all | solution.py:39
  42.5 4.1 %all-to-all-start.3 = ((f32[16,4,8,512]{3,2,1,0:T(8,128)}), f32[16,4,8,512]{3,2,1,0:T(8,128)S(1)}, u32[]{:S(2)}, u32[]{:S(2)}) async-start(f32[16,4,8,512]{3,2,1,0:T(8,128)} %copy.142), calls=%async_computation.3 | async-start | bytes 2097152 | tf_op jit(solution)/shard_map/all_to_all | solution.py:63
  52.1 4.4 %copy.128 = f32[16,4,8,2048]{3,2,1,0:T(8,128)} copy(f32[16,4,8,2048]{3,0,2,1:T(8,128)S(1)} %pad_maximum_fusion) | data formatting | bytes 8388608 | tf_op jit(solution)/shard_map/stack | solution.py:51
  56.5 13.8 %all-to-all-done.3 = f32[16,4,8,512]{3,2,1,0:T(8,128)S(1)} async-done(((f32[16,4,8,512]{3,2,1,0:T(8,128)}), f32[16,4,8,512]{3,2,1,0:T(8,128)S(1)}, u32[]{:S(2)}, u32[]{:S(2)}) %all-to-all-start.3) | async-done | bytes 1048608 | tf_op jit(solution)/shard_map/all_to_all | solution.py:63
  70.3 6.2 %all-to-all-start.1 = ((f32[16,4,8,2048]{3,2,1,0:T(8,128)}), f32[16,4,8,2048]{3,2,1,0:T(8,128)}, u32[]{:S(2)}, u32[]{:S(2)}) async-start(f32[16,4,8,2048]{3,2,1,0:T(8,128)} %copy.128), calls=%async_computation.1 | async-start | bytes 8388608 | tf_op jit(solution)/shard_map/all_to_all | solution.py:62
  85.1 68.9 %all-to-all-done.1 = f32[16,4,8,2048]{3,2,1,0:T(8,128)} async-done(((f32[16,4,8,2048]{3,2,1,0:T(8,128)}), f32[16,4,8,2048]{3,2,1,0:T(8,128)}, u32[]{:S(2)}, u32[]{:S(2)}) %all-to-all-start.1) | async-done | bytes 4194336 | tf_op jit(solution)/shard_map/all_to_all | solution.py:62
  154.0 2.7 fusion.334
  159.1 2.5 fusion.84
  161.7 2.3 fusion.86
  164.0 2.5 fusion.9
  166.5 3.2 multiply_subtract_fusion.2
  169.7 3.3 fusion.23
  173.0 3.5 fusion.19
  176.5 3.5 fusion.5
  180.6 4.7 %multiply_subtract_fusion.1 = (f32[2,16,8,2048]{3,2,1,0:T(8,128)S(1)}, f32[2,16,8,2048]{3,2,1,0:T(8,128)S(1)}) fusion(f32[2,16,8,2048]{3,2,1,0:T(8,128)S(1)} %bitcast.230, f32[2,16,8,2048]{3,2,1,0:T(8,128)S(1)} %fusion.5, f32[2,16,8,2048]{3,2,1,0:T(8,128)S(1)} %bitcast.229, f32[2,16,2048,8]{2,3,1,0:T(8,128)S(1)} %fusion.19, ...), kind=kOutput, calls=%fused_computation.37 | convolution fusion | flops 54526848 | bytes 14680064 | tf_op jit(solution)/shard_map/br,karc->kabc/dot_general | solution.py:18
  185.3 2.5 fusion.125
  187.7 2.0 fusion.127
  189.8 2.1 convolution_add_fusion.1
  191.9 2.6 subtract_bitcast_fusion
  194.5 3.2 fusion.17
  197.7 3.4 fusion.13
  201.1 3.2 fusion.1
  204.3 4.2 %multiply_subtract_fusion = (f32[2,16,8,2048]{3,1,2,0:T(8,128)S(1)}, f32[2,16,8,2048]{3,1,2,0:T(8,128)S(1)}) fusion(f32[2,16,8,2048]{3,1,2,0:T(8,128)S(1)} %fusion.1, f32[2,16,8]{1,2,0:T(8,128)S(1)} %get-tuple-element.33, f32[2,16,8]{1,2,0:T(8,128)S(1)} %get-tuple-element.35, f32[2,8,2048,16]{2,3,1,0:T(8,128)S(1)} %fusion.13, ...), kind=kOutput, calls=%fused_computation.33 | convolution fusion | flops 104336896 | bytes 10487808 | tf_op jit(solution)/shard_map/aq,karc->kqrc/dot_general | solution.py:18
  209.4 2.4 copy.174
  211.9 111.6 %all_to_all.48 = f32[16,4,8,2048]{3,2,1,0:T(8,128)S(1)} all-to-all(f32[16,4,8,2048]{3,2,1,0:T(8,128)S(1)} %copy.174), channel_id=1, replica_groups=mesh['seq'=16,'ch'=2] {'seq'}, dimensions={0} | all-to-all | bytes 8388608 | tf_op jit(solution)/shard_map/all_to_all | solution.py:115
  328.5 1.5 fusion.12
  330.7 29.2 %all_to_all.49 = f32[16,8,2048]{2,1,0:T(8,128)S(1)} all-to-all(f32[16,8,2048]{2,1,0:T(8,128)S(1)} %copy.179), channel_id=1, replica_groups=mesh['seq'=16,'ch'=2] {'seq'}, dimensions={0} | all-to-all | bytes 2097152 | tf_op jit(solution)/shard_map/all_to_all | solution.py:123
  (63 shorter events, 33.2 us)
Async XLA Ops:
  5.2 16.0 %all-to-all-start.2 = ((bf16[16,2,2048]{2,1,0:T(2,128)(2,1)}), bf16[16,2,2048]{2,1,0:T(2,128)(2,1)S(1)}, u32[]{:S(2)}, u32[]{:S(2)}) async-start(bf16[16,2,2048]{2,1,0:T(2,128)(2,1)} %reshape.185), calls=%async_computation.2 | async-start | bytes 262144 | tf_op jit(solution)/shard_map/all_to_all | solution.py:40
  21.2 21.2 %all-to-all-start = ((bf16[16,2,8192]{2,1,0:T(2,128)(2,1)}), bf16[16,2,8192]{2,1,0:T(2,128)(2,1)S(1)}, u32[]{:S(2)}, u32[]{:S(2)}) async-start(bf16[16,2,8192]{2,1,0:T(2,128)(2,1)} %reshape.183), calls=%async_computation | async-start | bytes 1048576 | tf_op jit(solution)/shard_map/all_to_all | solution.py:39
  42.5 27.8 %all-to-all-start.3 = ((f32[16,4,8,512]{3,2,1,0:T(8,128)}), f32[16,4,8,512]{3,2,1,0:T(8,128)S(1)}, u32[]{:S(2)}, u32[]{:S(2)}) async-start(f32[16,4,8,512]{3,2,1,0:T(8,128)} %copy.142), calls=%async_computation.3 | async-start | bytes 2097152 | tf_op jit(solution)/shard_map/all_to_all | solution.py:63
  70.3 83.8 %all-to-all-start.1 = ((f32[16,4,8,2048]{3,2,1,0:T(8,128)}), f32[16,4,8,2048]{3,2,1,0:T(8,128)}, u32[]{:S(2)}, u32[]{:S(2)}) async-start(f32[16,4,8,2048]{3,2,1,0:T(8,128)} %copy.128), calls=%async_computation.1 | async-start | bytes 8388608 | tf_op jit(solution)/shard_map/all_to_all | solution.py:62
  330.1 29.8 %copy-start = (bf16[128,2048]{1,0:T(8,128)(2,1)S(1)}, bf16[128,2048]{1,0:T(8,128)(2,1)}, u32[]{:S(2)}) copy-start(bf16[128,2048]{1,0:T(8,128)(2,1)} %param.7) | copy-start | bytes 1572868
  330.1 29.8 %copy-start.1 = (bf16[128,2048]{1,0:T(8,128)(2,1)S(1)}, bf16[128,2048]{1,0:T(8,128)(2,1)}, u32[]{:S(2)}) copy-start(bf16[128,2048]{1,0:T(8,128)(2,1)} %param.6) | copy-start | bytes 1572868
  330.1 29.8 %copy-start.2 = (bf16[128,2048]{1,0:T(8,128)(2,1)S(1)}, bf16[128,2048]{1,0:T(8,128)(2,1)}, u32[]{:S(2)}) copy-start(bf16[128,2048]{1,0:T(8,128)(2,1)} %param.5) | copy-start | bytes 1572868
  330.1 29.8 %copy-start.3 = (f32[2048]{0:T(1024)S(1)}, f32[2048]{0:T(1024)}, u32[]{:S(2)}) copy-start(f32[2048]{0:T(1024)} %param.9) | copy-start | bytes 24580
where the time goes:
time: 368 us; the launch traced here: 361 us
  blocking collectives  143 us (39%)
  waiting for transfers between devices  94.9 us (26%)
  matrix products  67.9 us (18%)
  starting transfers between devices  24.9 us (7%)
  local copies, waits for them, and re-layouts  20.5 us (6%)
  other arithmetic  9.16 us (2%)
    all_to_all x1, blocking collectives, four_step(): lax.all_to_all(parts_back, 'seq', split_axis=0, concat_axis=0, tiled=True)  112 us
    all_to_all x1, waiting for transfers between devices, four_step(): lax.all_to_all(send_parts(got_input), 'seq', split_axis=0, concat_axis=0,...  68.9 us
    dot_general x36, matrix products, contract(): return jnp.einsum(form, table, operand, precision=HIGHEST)  67.9 us
    all_to_all x1, blocking collectives, four_step(): lax.all_to_all(convolved, 'seq', split_axis=0, concat_axis=1, tiled=True)  29.2 us
    all_to_all x1, waiting for transfers between devices, four_step(): lax.all_to_all(send_parts(got_filter), 'seq', split_axis=0, concat_axis=0...  13.8 us
    all_to_all x1, waiting for transfers between devices, four_step(): lax.all_to_all(mixed_input[None], 'seq', split_axis=1, concat_axis=0, til...  11.6 us
    all_to_all x1, starting transfers between devices, four_step(): lax.all_to_all(filter_local[None], 'seq', split_axis=1, concat_axis=0, ti...  8.2 us
  transfers between devices with their start and end apart: 4, of which 4 were waited for; matrix products, arithmetic and copies ran while one was open for 8% of the time, Pallas kernels for 0%

commit v1 on v0

--- a/solution.py
+++ b/solution.py
@@ -1,8 +1,11 @@
+import functools
 import math
 
 import jax
 import jax.numpy as jnp
 from jax import lax
+from jax.experimental import pallas as pl
+from jax.experimental.pallas import tpu as pltpu
 from jax.sharding import PartitionSpec as P
 
 HIGHEST = lax.Precision.HIGHEST
@@ -136,9 +139,266 @@
     return gated.astype(jnp.bfloat16)
 
 
+LANES = 128
+MESH = pl.DeviceIdType.MESH
+
+
+def conv_kernel(
+    seq_count,
+    ch_count,
+    repeat,
+    outer_ref,
+    inner_ref,
+    values_ref,
+    taps_ref,
+    skip_ref,
+    out_ref,
+    mixed_ref,
+    taps_send,
+    taps_recv,
+    taps_wide,
+    send_ref,
+    recv_ref,
+    recv_wide,
+    padded_ref,
+    toeplitz_ref,
+    conv_wide,
+    back_send,
+    back_recv,
+    taps_sems,
+    send_sems,
+    back_sems,
+):
+    devices = seq_count * ch_count
+    per_dev = taps_send.shape[1]
+    members = ch_count * repeat
+    pairs = per_dev // 2
+    width = out_ref.shape[1]
+    seq_at = lax.axis_index("seq")
+    ch_at = lax.axis_index("ch")
+    me = seq_at * ch_count + ch_at
+
+    def partner(step):
+        flat = lax.rem(me + step, devices)
+        return lax.div(flat, ch_count), lax.rem(flat, ch_count)
+
+    barrier = pltpu.get_barrier_semaphore()
+
+    @pl.loop(1, devices)
+    def _(step):
+        to_seq, to_ch = partner(step)
+        pl.semaphore_signal(barrier, inc=1, device_id=(to_seq, to_ch), device_id_type=MESH)
+
+    taps_t = taps_ref[...].astype(jnp.float32).T.astype(jnp.bfloat16)
+    taps_send[...] = taps_t.reshape(taps_send.shape)
+
+    slots_per_block = LANES // per_dev
+    blocks_per_ch = seq_count // slots_per_block
+
+    @pl.loop(0, width // LANES)
+    def _(block):
+        lanes = pl.ds(pl.multiple_of(block * LANES, LANES), LANES)
+        product = inner_ref[:, lanes].astype(jnp.float32) * values_ref[:, lanes].astype(jnp.float32)
+        mixed = product.astype(jnp.bfloat16)
+        mixed_ref[:, lanes] = mixed
+        turned = mixed.astype(jnp.float32).T.astype(jnp.bfloat16)
+        rep = block // (ch_count * blocks_per_ch)
+        rest = lax.rem(block, ch_count * blocks_per_ch)
+        to_ch = rest // blocks_per_ch
+        slot = lax.rem(rest, blocks_per_ch) * slots_per_block
+        send_ref[rep, to_ch, pl.ds(slot, slots_per_block)] = turned.reshape(
+            slots_per_block, per_dev, LANES
+        )
+
+    pl.semaphore_wait(barrier, devices - 1)
+
+    own_taps = pltpu.make_async_copy(taps_send.at[seq_at], taps_recv.at[seq_at], taps_sems.at[1])
+    own_taps.start()
+
+    @pl.loop(1, seq_count)
+    def _(step):
+        to_seq = lax.rem(seq_at + step, seq_count)
+        pltpu.make_async_remote_copy(
+            src_ref=taps_send.at[to_seq],
+            dst_ref=taps_recv.at[seq_at],
+            send_sem=taps_sems.at[0],
+            recv_sem=taps_sems.at[1],
+            device_id=(to_seq, ch_at),
+            device_id_type=MESH,
+        ).start()
+
+    own = pltpu.make_async_copy(send_ref.at[:, ch_at, seq_at], recv_ref.at[me], send_sems.at[1])
+    own.start()
+
+    @pl.loop(1, devices)
+    def _(step):
+        to_seq, to_ch = partner(step)
+        pltpu.make_async_remote_copy(
+            src_ref=send_ref.at[:, to_ch, to_seq],
+            dst_ref=recv_ref.at[me],
+            send_sem=send_sems.at[0],
+            recv_sem=send_sems.at[1],
+            device_id=(to_seq, to_ch),
+            device_id_type=MESH,
+        ).start()
+
+    pltpu.make_async_copy(taps_recv, taps_recv, taps_sems.at[1]).wait()
+    taps_wide[...] = taps_recv[...].reshape(taps_wide.shape).astype(jnp.float32)
+    row = lax.broadcasted_iota(jnp.int32, (LANES, LANES), 0)
+    col = lax.broadcasted_iota(jnp.int32, (LANES, LANES), 1)
+    upper = col >= row
+
+    @pl.loop(0, pairs)
+    def _(pair):
+        for half in range(2):
+
+            def block_step(lag, before):
+                line = taps_wide[pl.ds(lag * per_dev + pair * 2 + half, 1), :]
+                spread = jnp.broadcast_to(line, (LANES, LANES))
+                rolled = pltpu.roll(spread, 0, 1, stride=1, stride_axis=0)
+                toeplitz_ref[
+                    pair,
+                    pl.ds(pl.multiple_of(lag * LANES, LANES), LANES),
+                    half * LANES : (half + 1) * LANES,
+                ] = jnp.where(upper, rolled, before).astype(jnp.bfloat16)
+                return rolled
+
+            lax.fori_loop(0, seq_count, block_step, jnp.zeros((LANES, LANES), jnp.float32))
+
+    group = 2 * members
+    padded_ref[:, 0 : seq_count * group, :] = jnp.zeros(
+        (pairs, seq_count * group, LANES), jnp.bfloat16
+    )
+
+    pltpu.make_async_copy(recv_ref, recv_ref, send_sems.at[1]).wait()
+    block_rows = members * per_dev
+    recv_wide[...] = recv_ref[...].reshape(recv_wide.shape).astype(jnp.float32)
+
+    @pl.loop(0, seq_count)
+    def _(place):
+        for pair in range(pairs):
+            first = recv_wide[pl.ds(place * block_rows + 2 * pair, members, stride=per_dev), :]
+            second = recv_wide[pl.ds(place * block_rows + 2 * pair + 1, members, stride=per_dev), :]
+            padded_ref[pair, pl.ds(pl.multiple_of((seq_count + place) * group, group), group), :] = (
+                jnp.concatenate([first, second], axis=0).astype(jnp.bfloat16)
+            )
+
+    @pl.loop(0, pairs)
+    def _(pair):
+        left = jnp.concatenate(
+            [
+                padded_ref[pair, (seq_count - lag) * group : (2 * seq_count - lag) * group, :]
+                for lag in range(seq_count)
+            ],
+            axis=1,
+        )
+        total = jnp.dot(left, toeplitz_ref[pair], preferred_element_type=jnp.float32)
+        for place in range(seq_count):
+            for half in range(2):
+                top = place * group + half * members
+                conv_wide[
+                    pl.ds(place * block_rows + 2 * pair + half, members, stride=per_dev), :
+                ] = total[top : top + members, half * LANES : (half + 1) * LANES]
+
+    back_send[...] = conv_wide[...].astype(jnp.bfloat16).reshape(back_send.shape)
+
+    own_back = pltpu.make_async_copy(
+        back_send.at[me], back_recv.at[:, ch_at, seq_at], back_sems.at[1]
+    )
+    own_back.start()
+
+    @pl.loop(1, devices)
+    def _(step):
+        to_seq, to_ch = partner(step)
+        pltpu.make_async_remote_copy(
+            src_ref=back_send.at[to_seq * ch_count + to_ch],
+            dst_ref=back_recv.at[:, ch_at, seq_at],
+            send_sem=back_sems.at[0],
+            recv_sem=back_sems.at[1],
+            device_id=(to_seq, to_ch),
+            device_id_type=MESH,
+        ).start()
+
+    pltpu.make_async_copy(back_recv, back_recv, back_sems.at[1]).wait()
+
+    @pl.loop(0, width // LANES)
+    def _(block):
+        lanes = pl.ds(pl.multiple_of(block * LANES, LANES), LANES)
+        rep = block // (ch_count * blocks_per_ch)
+        rest = lax.rem(block, ch_count * blocks_per_ch)
+        from_ch = rest // blocks_per_ch
+        slot = lax.rem(rest, blocks_per_ch) * slots_per_block
+        got = back_recv[rep, from_ch, pl.ds(slot, slots_per_block)]
+        convolved = got.reshape(LANES, LANES).astype(jnp.float32).T
+        mixed = mixed_ref[:, lanes].astype(jnp.float32)
+        gated = outer_ref[:, lanes].astype(jnp.float32) * (convolved + skip_ref[:, lanes] * mixed)
+        out_ref[:, lanes] = gated.astype(jnp.bfloat16)
+
+    others = pl.ds(0, devices - 1)
+    seq_others = pl.ds(0, seq_count - 1)
+    pltpu.make_async_copy(
+        taps_recv.at[seq_others], taps_recv.at[seq_others], taps_sems.at[0]
+    ).wait()
+    pltpu.make_async_copy(recv_ref.at[others], recv_ref.at[others], send_sems.at[0]).wait()
+    pltpu.make_async_copy(back_send.at[others], back_send.at[others], back_sems.at[0]).wait()
+
+
+def fused(gate_outer, gate_inner, values_in, filter_taps, skip_gain):
+    seq_count = lax.axis_size("seq")
+    ch_count = lax.axis_size("ch")
+    length_dev, width = gate_outer.shape
+    filters = filter_taps.shape[1]
+    per_dev = filters // seq_count
+    repeat = width // (filters * ch_count)
+    devices = seq_count * ch_count
+    pairs = per_dev // 2
+    members = ch_count * repeat
+    length = seq_count * length_dev
+    bf16, f32 = jnp.bfloat16, jnp.float32
+    return pl.pallas_call(
+        functools.partial(conv_kernel, seq_count, ch_count, repeat),
+        out_shape=jax.ShapeDtypeStruct((length_dev, width), bf16),
+        in_specs=[pl.BlockSpec(memory_space=pltpu.VMEM)] * 5,
+        out_specs=pl.BlockSpec(memory_space=pltpu.VMEM),
+        scratch_shapes=[
+            pltpu.VMEM((length_dev, width), bf16),
+            pltpu.VMEM((seq_count, per_dev, LANES), bf16),
+            pltpu.VMEM((seq_count, per_dev, LANES), bf16),
+            pltpu.VMEM((seq_count * per_dev, LANES), f32),
+            pltpu.VMEM((repeat, ch_count, seq_count, per_dev, LANES), bf16),
+            pltpu.VMEM((devices, repeat, per_dev, LANES), bf16),
+            pltpu.VMEM((width, LANES), f32),
+            pltpu.VMEM((pairs, 2 * seq_count * 2 * members, LANES), bf16),
+            pltpu.VMEM((pairs, length, 2 * LANES), bf16),
+            pltpu.VMEM((width, LANES), f32),
+            pltpu.VMEM((devices, repeat, per_dev, LANES), bf16),
+            pltpu.VMEM((repeat, ch_count, seq_count, per_dev, LANES), bf16),
+            pltpu.SemaphoreType.DMA((2,)),
+            pltpu.SemaphoreType.DMA((2,)),
+            pltpu.SemaphoreType.DMA((2,)),
+        ],
+        compiler_params=pltpu.CompilerParams(
+            collective_id=0, has_side_effects=True, vmem_limit_bytes=40 * 1024 * 1024
+        ),
+    )(gate_outer, gate_inner, values_in, filter_taps, skip_gain[None, :])
+
+
+def whole_filters(gate_outer, filter_taps):
+    seq_count = lax.axis_size("seq")
+    length_dev, width = gate_outer.shape
+    per_dev = filter_taps.shape[1] // seq_count
+    members = width // filter_taps.shape[1]
+    return length_dev == LANES and per_dev % 16 == 0 and LANES % per_dev == 0 and members == 8
+
+
+def per_device(gate_outer, gate_inner, values_in, filter_taps, skip_gain):
+    run = fused if whole_filters(gate_outer, filter_taps) else on_device
+    return run(gate_outer, gate_inner, values_in, filter_taps, skip_gain)
+
+
 def solution(mesh):
     return jax.shard_map(
-        on_device,
+        per_device,
         mesh=mesh,
         in_specs=(P("seq", "ch"), P("seq", "ch"), P("seq", "ch"), P("seq", "ch"), P("ch")),
         out_specs=P("seq", "ch"),

time: 368 us -> 56.5 us (0.15)
  the two profiles are of different devices: /device:TPU:0 before, /device:TPU:25 now
where the time goes in v1:
time: 56.5 us; the launch traced here: 56.2 us
  Pallas kernels  50.7 us (90%)
  local copies, waits for them, and re-layouts  5.45 us (10%)
    pallas_call x1, Pallas kernels, fused(): pl.pallas_call(functools.partial(conv_kernel, seq_count, ch_count, repeat...  50.7 us
    unnamed x11, local copies, waits for them, and re-layouts  5.45 us

profile of v1, /device:TPU:25, one launch (start us, length us, event | category | flops | bytes accessed | tf_op | source)
XLA Modules:
  0.0 56.2 jit_solution(13318899846050009241)
XLA Ops:
  0.0 0.0 copy-start
  0.0 1.0 %copy-done = bf16[128,2048]{1,0:T(8,128)(2,1)S(1)} copy-done((bf16[128,2048]{1,0:T(8,128)(2,1)S(1)}, bf16[128,2048]{1,0:T(8,128)(2,1)}, u32[]{:S(2)}) %copy-start) | copy-done | bytes 524312
  1.0 0.0 copy-start.1
  1.0 1.0 %copy-done.1 = bf16[128,2048]{1,0:T(8,128)(2,1)S(1)} copy-done((bf16[128,2048]{1,0:T(8,128)(2,1)S(1)}, bf16[128,2048]{1,0:T(8,128)(2,1)}, u32[]{:S(2)}) %copy-start.1) | copy-done | bytes 524312
  2.1 0.0 copy-start.2
  2.1 1.0 %copy-done.2 = bf16[128,2048]{1,0:T(8,128)(2,1)S(1)} copy-done((bf16[128,2048]{1,0:T(8,128)(2,1)S(1)}, bf16[128,2048]{1,0:T(8,128)(2,1)}, u32[]{:S(2)}) %copy-start.2) | copy-done | bytes 524312
  3.1 0.0 copy-start.3
  3.1 0.8 %copy-done.3 = bf16[128,256]{1,0:T(8,128)(2,1)S(1)} copy-done((bf16[128,256]{1,0:T(8,128)(2,1)S(1)}, bf16[128,256]{1,0:T(8,128)(2,1)}, u32[]{:S(2)}) %copy-start.3) | copy-done | bytes 65560
  4.0 0.0 copy-start.4
  4.0 0.7 %copy-done.4 = f32[2048]{0:T(1024)S(1)} copy-done((f32[2048]{0:T(1024)S(1)}, f32[2048]{0:T(1024)}, u32[]{:S(2)}) %copy-start.4) | copy-done | bytes 8216
  4.7 50.7 %shard_map.55 = bf16[128,2048]{1,0:T(8,128)(2,1)S(1)} custom-call(bf16[128,2048]{1,0:T(8,128)(2,1)S(1)} %copy-done, bf16[128,2048]{1,0:T(8,128)(2,1)S(1)} %copy-done.1, bf16[128,2048]{1,0:T(8,128)(2,1)S(1)} %copy-done.2, bf16[128,256]{1,0:T(8,128)(2,1)S(1)} %copy-done.3, f32[1,2048]{1,0:T(1,128)S(1)} %bitcast.1), custom_call_target="tpu_custom_call" | custom-call | tf_op jit(solution)/shard_map/pallas_call | solution.py:358
  55.4 0.8 %copy.7 = bf16[128,2048]{1,0:T(8,128)(2,1)} copy(bf16[128,2048]{1,0:T(8,128)(2,1)S(1)} %shard_map.55) | data formatting | bytes 1048576
Async XLA Ops:
  0.0 1.0 %copy-start = (bf16[128,2048]{1,0:T(8,128)(2,1)S(1)}, bf16[128,2048]{1,0:T(8,128)(2,1)}, u32[]{:S(2)}) copy-start(bf16[128,2048]{1,0:T(8,128)(2,1)} %outer_ref.1) | copy-start | bytes 1572868
  1.0 1.0 %copy-start.1 = (bf16[128,2048]{1,0:T(8,128)(2,1)S(1)}, bf16[128,2048]{1,0:T(8,128)(2,1)}, u32[]{:S(2)}) copy-start(bf16[128,2048]{1,0:T(8,128)(2,1)} %inner_ref.1) | copy-start | bytes 1572868
  2.1 1.0 %copy-start.2 = (bf16[128,2048]{1,0:T(8,128)(2,1)S(1)}, bf16[128,2048]{1,0:T(8,128)(2,1)}, u32[]{:S(2)}) copy-start(bf16[128,2048]{1,0:T(8,128)(2,1)} %values_ref.1) | copy-start | bytes 1572868
  3.1 0.8 %copy-start.3 = (bf16[128,256]{1,0:T(8,128)(2,1)S(1)}, bf16[128,256]{1,0:T(8,128)(2,1)}, u32[]{:S(2)}) copy-start(bf16[128,256]{1,0:T(8,128)(2,1)} %taps_ref.1) | copy-start | bytes 196612
  4.0 0.7 %copy-start.4 = (f32[2048]{0:T(1024)S(1)}, f32[2048]{0:T(1024)}, u32[]{:S(2)}) copy-start(f32[2048]{0:T(1024)} %param.9) | copy-start | bytes 24580

commit v2 on v0

--- a/solution.py
+++ b/solution.py
@@ -1,8 +1,11 @@
+import functools
 import math
 
 import jax
 import jax.numpy as jnp
 from jax import lax
+from jax.experimental import pallas as pl
+from jax.experimental.pallas import tpu as pltpu
 from jax.sharding import PartitionSpec as P
 
 HIGHEST = lax.Precision.HIGHEST
@@ -136,9 +139,315 @@
     return gated.astype(jnp.bfloat16)
 
 
+LANES = 128
+HALF_ROWS = 8
+MESH = pl.DeviceIdType.MESH
+
+
+def conv_kernel(
+    seq_count,
+    ch_count,
+    repeat,
+    outer_hbm,
+    inner_hbm,
+    values_hbm,
+    taps_hbm,
+    skip_hbm,
+    out_ref,
+    outer_ref,
+    inner_ref,
+    values_ref,
+    taps_ref,
+    skip_ref,
+    mixed_ref,
+    taps_send,
+    taps_recv,
+    taps_wide,
+    send_ref,
+    recv_ref,
+    recv_wide,
+    padded_ref,
+    toeplitz_ref,
+    conv_wide,
+    back_send,
+    back_recv,
+    load_sems,
+    taps_sems,
+    send_sems,
+    back_sems,
+):
+    devices = seq_count * ch_count
+    members = ch_count * repeat
+    pairs = HALF_ROWS // 2
+    bf16, f32 = jnp.bfloat16, jnp.float32
+    seq_at = lax.axis_index("seq")
+    ch_at = lax.axis_index("ch")
+    me = seq_at * ch_count + ch_at
+
+    loads = [
+        pltpu.make_async_copy(source, target, load_sems.at[at])
+        for at, (source, target) in enumerate(
+            [
+                (taps_hbm, taps_ref),
+                (inner_hbm, inner_ref),
+                (values_hbm, values_ref),
+                (outer_hbm, outer_ref),
+                (skip_hbm, skip_ref),
+            ]
+        )
+    ]
+    for load in loads:
+        load.start()
+
+    def partner(step):
+        offset = devices // 2 + step // 2 * (2 * (step % 2) - 1)
+        flat = lax.rem(me + offset, devices)
+        return flat // ch_count, lax.rem(flat, ch_count)
+
+    barrier = pltpu.get_barrier_semaphore()
+
+    @pl.loop(1, devices)
+    def _(step):
+        to_seq, to_ch = partner(step)
+        pl.semaphore_signal(barrier, inc=1, device_id=(to_seq, to_ch), device_id_type=MESH)
+
+    def lanes_of(rep, to_ch, half):
+        return pl.ds(((rep * ch_count + to_ch) * 2 + half) * LANES, LANES)
+
+    def interleave(first, second):
+        shape = (seq_count, 1, HALF_ROWS, LANES)
+        both = jnp.concatenate([first.reshape(shape), second.reshape(shape)], axis=1)
+        return both.reshape(seq_count, 2 * HALF_ROWS, LANES).astype(bf16)
+
+    def mix(half):
+        for duo in range(repeat // 2):
+            for to_ch in range(ch_count):
+                turned = []
+                for rep in (2 * duo, 2 * duo + 1):
+                    lanes = lanes_of(rep, to_ch, half)
+                    product = inner_ref[:, lanes].astype(f32) * values_ref[:, lanes].astype(f32)
+                    mixed = product.astype(bf16)
+                    mixed_ref[:, lanes] = mixed
+                    turned.append(mixed.astype(f32).T)
+                send_ref[half, duo, to_ch] = interleave(*turned)
+
+    loads[0].wait()
+    taps_t = taps_ref[...].astype(f32).T
+    taps_send[...] = interleave(taps_t[:LANES], taps_t[LANES:])
+    loads[1].wait()
+    loads[2].wait()
+    mix(0)
+
+    pl.semaphore_wait(barrier, devices - 1)
+
+    pltpu.make_async_copy(taps_send.at[seq_at], taps_recv.at[seq_at], taps_sems.at[1]).start()
+
+    @pl.loop(1, seq_count)
+    def _(step):
+        to_seq = lax.rem(seq_at + step, seq_count)
+        pltpu.make_async_remote_copy(
+            src_ref=taps_send.at[to_seq],
+            dst_ref=taps_recv.at[seq_at],
+            send_sem=taps_sems.at[0],
+            recv_sem=taps_sems.at[1],
+            device_id=(to_seq, ch_at),
+            device_id_type=MESH,
+        ).start()
+
+    def send_out(half):
+        pltpu.make_async_copy(
+            send_ref.at[half, :, ch_at, seq_at], recv_ref.at[half, me], send_sems.at[1, half]
+        ).start()
+
+        @pl.loop(1, devices)
+        def _(step):
+            to_seq, to_ch = partner(step)
+            pltpu.make_async_remote_copy(
+                src_ref=send_ref.at[half, :, to_ch, to_seq],
+                dst_ref=recv_ref.at[half, me],
+                send_sem=send_sems.at[0, half],
+                recv_sem=send_sems.at[1, half],
+                device_id=(to_seq, to_ch),
+                device_id_type=MESH,
+            ).start()
+
+    send_out(0)
+    mix(1)
+    send_out(1)
+
+    group = 2 * members
+    padded_ref[:, 0 : seq_count * group, :] = jnp.zeros((pairs, seq_count * group, LANES), bf16)
+
+    pltpu.make_async_copy(taps_recv, taps_recv, taps_sems.at[1]).wait()
+    taps_wide[...] = taps_recv[...].reshape(taps_wide.shape).astype(f32)
+    row = lax.broadcasted_iota(jnp.int32, (LANES, LANES), 0)
+    col = lax.broadcasted_iota(jnp.int32, (LANES, LANES), 1)
+    upper = col >= row
+
+    @pl.loop(0, 2 * pairs)
+    def _(pair):
+        for side in range(2):
+            before = jnp.zeros((LANES, LANES), f32)
+            for lag in range(seq_count):
+                line = taps_wide[pl.ds(lag * 2 * HALF_ROWS + pair * 2 + side, 1), :]
+                spread = jnp.broadcast_to(line, (LANES, LANES))
+                rolled = pltpu.roll(spread, 0, 1, stride=1, stride_axis=0)
+                toeplitz_ref[
+                    pair, lag * LANES : (lag + 1) * LANES, side * LANES : (side + 1) * LANES
+                ] = jnp.where(upper, rolled, before).astype(bf16)
+                before = rolled
+
+    block_rows = members * HALF_ROWS
+
+    def convolve(half):
+        pltpu.make_async_copy(recv_ref.at[half], recv_ref.at[half], send_sems.at[1, half]).wait()
+        recv_wide[...] = recv_ref[half].reshape(recv_wide.shape).astype(f32)
+
+        @pl.loop(0, seq_count)
+        def _(place):
+            for pair in range(pairs):
+                rows = [
+                    recv_wide[
+                        pl.ds(place * block_rows + 2 * pair + side, members, stride=HALF_ROWS), :
+                    ]
+                    for side in range(2)
+                ]
+                padded_ref[
+                    pair, pl.ds(pl.multiple_of((seq_count + place) * group, group), group), :
+                ] = jnp.concatenate(rows, axis=0).astype(bf16)
+
+        @pl.loop(0, pairs)
+        def _(pair):
+            left = jnp.concatenate(
+                [
+                    padded_ref[pair, (seq_count - lag) * group : (2 * seq_count - lag) * group, :]
+                    for lag in range(seq_count)
+                ],
+                axis=1,
+            )
+            total = jnp.dot(left, toeplitz_ref[half * pairs + pair], preferred_element_type=f32)
+            for place in range(seq_count):
+                for side in range(2):
+                    top = place * group + side * members
+                    conv_wide[
+                        pl.ds(place * block_rows + 2 * pair + side, members, stride=HALF_ROWS), :
+                    ] = total[top : top + members, side * LANES : (side + 1) * LANES]
+
+        back_send[half] = conv_wide[...].astype(bf16).reshape(back_send.shape[1:])
+        pltpu.make_async_copy(
+            back_send.at[half, me], back_recv.at[half, :, ch_at, seq_at], back_sems.at[1, half]
+        ).start()
+
+        @pl.loop(1, devices)
+        def _(step):
+            to_seq, to_ch = partner(step)
+            pltpu.make_async_remote_copy(
+                src_ref=back_send.at[half, to_seq * ch_count + to_ch],
+                dst_ref=back_recv.at[half, :, ch_at, seq_at],
+                send_sem=back_sems.at[0, half],
+                recv_sem=back_sems.at[1, half],
+                device_id=(to_seq, to_ch),
+                device_id_type=MESH,
+            ).start()
+
+    convolve(0)
+    convolve(1)
+
+    def gate(half):
+        pltpu.make_async_copy(back_recv.at[half], back_recv.at[half], back_sems.at[1, half]).wait()
+        for duo in range(repeat // 2):
+            for from_ch in range(ch_count):
+                got = back_recv[half, duo, from_ch].astype(f32)
+                got = got.reshape(seq_count, 2, HALF_ROWS, LANES)
+                for side in range(2):
+                    lanes = lanes_of(2 * duo + side, from_ch, half)
+                    convolved = got[:, side].reshape(LANES, LANES).T
+                    mixed = mixed_ref[:, lanes].astype(f32)
+                    gated = outer_ref[:, lanes].astype(f32) * (
+                        convolved + skip_ref[:, lanes] * mixed
+                    )
+                    out_ref[:, lanes] = gated.astype(bf16)
+
+    loads[3].wait()
+    loads[4].wait()
+    gate(0)
+    gate(1)
+
+    seq_others = taps_recv.at[pl.ds(0, seq_count - 1)]
+    pltpu.make_async_copy(seq_others, seq_others, taps_sems.at[0]).wait()
+    for half in range(2):
+        others = recv_ref.at[half, pl.ds(0, devices - 1)]
+        pltpu.make_async_copy(others, others, send_sems.at[0, half]).wait()
+        others = back_send.at[half, pl.ds(0, devices - 1)]
+        pltpu.make_async_copy(others, others, back_sems.at[0, half]).wait()
+
+
+def fused(gate_outer, gate_inner, values_in, filter_taps, skip_gain):
+    seq_count = lax.axis_size("seq")
+    ch_count = lax.axis_size("ch")
+    length_dev, width = gate_outer.shape
+    filters = filter_taps.shape[1]
+    repeat = width // (filters * ch_count)
+    devices = seq_count * ch_count
+    pairs = HALF_ROWS // 2
+    group = 2 * ch_count * repeat
+    length = seq_count * length_dev
+    tile = 2 * HALF_ROWS
+    bf16, f32 = jnp.bfloat16, jnp.float32
+    return pl.pallas_call(
+        functools.partial(conv_kernel, seq_count, ch_count, repeat),
+        out_shape=jax.ShapeDtypeStruct((length_dev, width), bf16),
+        in_specs=[pl.BlockSpec(memory_space=pltpu.HBM)] * 5,
+        out_specs=pl.BlockSpec(memory_space=pltpu.VMEM),
+        scratch_shapes=[
+            pltpu.VMEM((length_dev, width), bf16),
+            pltpu.VMEM((length_dev, width), bf16),
+            pltpu.VMEM((length_dev, width), bf16),
+            pltpu.VMEM((length_dev, filters), bf16),
+            pltpu.VMEM((1, width), f32),
+            pltpu.VMEM((length_dev, width), bf16),
+            pltpu.VMEM((seq_count, tile, LANES), bf16),
+            pltpu.VMEM((seq_count, tile, LANES), bf16),
+            pltpu.VMEM((seq_count * tile, LANES), f32),
+            pltpu.VMEM((2, repeat // 2, ch_count, seq_count, tile, LANES), bf16),
+            pltpu.VMEM((2, devices, repeat // 2, tile, LANES), bf16),
+            pltpu.VMEM((width // 2, LANES), f32),
+            pltpu.VMEM((pairs, 2 * seq_count * group, LANES), bf16),
+            pltpu.VMEM((2 * pairs, length, 2 * LANES), bf16),
+            pltpu.VMEM((width // 2, LANES), f32),
+            pltpu.VMEM((2, devices, repeat // 2, tile, LANES), bf16),
+            pltpu.VMEM((2, repeat // 2, ch_count, seq_count, tile, LANES), bf16),
+            pltpu.SemaphoreType.DMA((5,)),
+            pltpu.SemaphoreType.DMA((2,)),
+            pltpu.SemaphoreType.DMA((2, 2)),
+            pltpu.SemaphoreType.DMA((2, 2)),
+        ],
+        compiler_params=pltpu.CompilerParams(
+            collective_id=0, has_side_effects=True, vmem_limit_bytes=40 * 1024 * 1024
+        ),
+    )(gate_outer, gate_inner, values_in, filter_taps, skip_gain[None, :])
+
+
+def whole_filters(gate_outer, filter_taps):
+    seq_count = lax.axis_size("seq")
+    length_dev, width = gate_outer.shape
+    filters = filter_taps.shape[1]
+    return (
+        length_dev == LANES
+        and filters == 2 * LANES
+        and seq_count * HALF_ROWS == LANES
+        and width == 8 * filters
+    )
+
+
+def per_device(gate_outer, gate_inner, values_in, filter_taps, skip_gain):
+    run = fused if whole_filters(gate_outer, filter_taps) else on_device
+    return run(gate_outer, gate_inner, values_in, filter_taps, skip_gain)
+
+
 def solution(mesh):
     return jax.shard_map(
-        on_device,
+        per_device,
         mesh=mesh,
         in_specs=(P("seq", "ch"), P("seq", "ch"), P("seq", "ch"), P("seq", "ch"), P("ch")),
         out_specs=P("seq", "ch"),

time: 368 us -> 40.2 us (0.11); the launches traced: 361 us -> 39.8 us
  blocking collectives: 143 us -> 0 us
  waiting for transfers between devices: 94.9 us -> 0 us
  matrix products: 67.9 us -> 0 us
  Pallas kernels: 0 us -> 34.4 us
  starting transfers between devices: 24.9 us -> 0 us
  local copies, waits for them, and re-layouts: 20.5 us -> 5.45 us
  other arithmetic: 9.16 us -> 0 us
    all_to_all x2 -> x0, blocking collectives: 141 us -> none  [the longest x1 112 us: four_step(): lax.all_to_all(parts_back, 'seq', split_axis=0, concat_axis=0, tiled=True)]
    all_to_all x4 -> x0, waiting for transfers between devices: 94.9 us -> none  [the longest x1 68.9 us: four_step(): lax.all_to_all(send_parts(got_input), 'seq', split_axis=0, concat_axis=0,...]
    dot_general x36 -> x0, matrix products: 67.9 us -> none  [contract(): return jnp.einsum(form, table, operand, precision=HIGHEST)]
    pallas_call x0 -> x1, Pallas kernels: none -> 34.4 us  [fused(): pl.pallas_call(functools.partial(conv_kernel, seq_count, ch_count, repeat...]
    all_to_all x4 -> x0, starting transfers between devices: 24.9 us -> none  [the longest x1 8.2 us: four_step(): lax.all_to_all(filter_local[None], 'seq', split_axis=1, concat_axis=0, ti...]
    another operation x10 -> x0, local copies, waits for them, and re-layouts: 11.9 us -> none  [the longest x2 5.97 us: send_parts(): jnp.stack([contract('dp,prc->drc', cos_first, received), -contract('dp,pr...]
    unnamed x2 -> x0, other arithmetic: 5.11 us -> none
  transfers between devices with their start and end apart: 4 -> 0, of which waited for: 4 -> 0; matrix products, arithmetic and copies ran while one was open for 8% -> 0% of each run, Pallas kernels for 0% -> 0%
where the time goes in v2:
time: 40.2 us; the launch traced here: 39.8 us
  Pallas kernels  34.4 us (86%)
  local copies, waits for them, and re-layouts  5.45 us (14%)
    pallas_call x1, Pallas kernels, fused(): pl.pallas_call(functools.partial(conv_kernel, seq_count, ch_count, repeat...  34.4 us
    unnamed x11, local copies, waits for them, and re-layouts  5.45 us

profile of v2, /device:TPU:0, one launch (start us, length us, event | category | flops | bytes accessed | tf_op | source)
XLA Modules:
  0.0 39.8 jit_solution(13323723082648434595)
XLA Ops:
  0.0 0.0 copy-start
  0.0 1.0 %copy-done = bf16[128,2048]{1,0:T(8,128)(2,1)S(1)} copy-done((bf16[128,2048]{1,0:T(8,128)(2,1)S(1)}, bf16[128,2048]{1,0:T(8,128)(2,1)}, u32[]{:S(2)}) %copy-start) | copy-done | bytes 524312
  1.0 0.0 copy-start.1
  1.0 1.0 %copy-done.1 = bf16[128,2048]{1,0:T(8,128)(2,1)S(1)} copy-done((bf16[128,2048]{1,0:T(8,128)(2,1)S(1)}, bf16[128,2048]{1,0:T(8,128)(2,1)}, u32[]{:S(2)}) %copy-start.1) | copy-done | bytes 524312
  2.1 0.0 copy-start.2
  2.1 1.0 %copy-done.2 = bf16[128,2048]{1,0:T(8,128)(2,1)S(1)} copy-done((bf16[128,2048]{1,0:T(8,128)(2,1)S(1)}, bf16[128,2048]{1,0:T(8,128)(2,1)}, u32[]{:S(2)}) %copy-start.2) | copy-done | bytes 524312
  3.1 0.0 copy-start.3
  3.1 0.8 %copy-done.3 = bf16[128,256]{1,0:T(8,128)(2,1)S(1)} copy-done((bf16[128,256]{1,0:T(8,128)(2,1)S(1)}, bf16[128,256]{1,0:T(8,128)(2,1)}, u32[]{:S(2)}) %copy-start.3) | copy-done | bytes 65560
  4.0 0.0 copy-start.4
  4.0 0.7 %copy-done.4 = f32[2048]{0:T(1024)S(1)} copy-done((f32[2048]{0:T(1024)S(1)}, f32[2048]{0:T(1024)}, u32[]{:S(2)}) %copy-start.4) | copy-done | bytes 8216
  4.7 34.4 %shard_map.55 = bf16[128,2048]{1,0:T(8,128)(2,1)S(1)} custom-call(bf16[128,2048]{1,0:T(8,128)(2,1)S(1)} %copy-done, bf16[128,2048]{1,0:T(8,128)(2,1)S(1)} %copy-done.1, bf16[128,2048]{1,0:T(8,128)(2,1)S(1)} %copy-done.2, bf16[128,256]{1,0:T(8,128)(2,1)S(1)} %copy-done.3, f32[1,2048]{1,0:T(1,128)S(1)} %bitcast.1), custom_call_target="tpu_custom_call" | custom-call | tf_op jit(solution)/shard_map/pallas_call | solution.py:397
  39.0 0.8 %copy.7 = bf16[128,2048]{1,0:T(8,128)(2,1)} copy(bf16[128,2048]{1,0:T(8,128)(2,1)S(1)} %shard_map.55) | data formatting | bytes 1048576
Async XLA Ops:
  0.0 1.0 %copy-start = (bf16[128,2048]{1,0:T(8,128)(2,1)S(1)}, bf16[128,2048]{1,0:T(8,128)(2,1)}, u32[]{:S(2)}) copy-start(bf16[128,2048]{1,0:T(8,128)(2,1)} %outer_hbm.1) | copy-start | bytes 1572868
  1.0 1.0 %copy-start.1 = (bf16[128,2048]{1,0:T(8,128)(2,1)S(1)}, bf16[128,2048]{1,0:T(8,128)(2,1)}, u32[]{:S(2)}) copy-start(bf16[128,2048]{1,0:T(8,128)(2,1)} %inner_hbm.1) | copy-start | bytes 1572868
  2.1 1.0 %copy-start.2 = (bf16[128,2048]{1,0:T(8,128)(2,1)S(1)}, bf16[128,2048]{1,0:T(8,128)(2,1)}, u32[]{:S(2)}) copy-start(bf16[128,2048]{1,0:T(8,128)(2,1)} %values_hbm.1) | copy-start | bytes 1572868
  3.1 0.8 %copy-start.3 = (bf16[128,256]{1,0:T(8,128)(2,1)S(1)}, bf16[128,256]{1,0:T(8,128)(2,1)}, u32[]{:S(2)}) copy-start(bf16[128,256]{1,0:T(8,128)(2,1)} %taps_hbm.1) | copy-start | bytes 196612
  4.0 0.7 %copy-start.4 = (f32[2048]{0:T(1024)S(1)}, f32[2048]{0:T(1024)}, u32[]{:S(2)}) copy-start(f32[2048]{0:T(1024)} %param.9) | copy-start | bytes 24580

commit v3 on v2

--- a/solution.py
+++ b/solution.py
@@ -153,6 +153,7 @@
     values_hbm,
     taps_hbm,
     skip_hbm,
+    out_hbm,
     out_ref,
     outer_ref,
     inner_ref,
@@ -175,6 +176,7 @@
     taps_sems,
     send_sems,
     back_sems,
+    store_sems,
 ):
     devices = seq_count * ch_count
     members = ch_count * repeat
@@ -353,6 +355,8 @@
     convolve(0)
     convolve(1)
 
+    stores = []
+
     def gate(half):
         pltpu.make_async_copy(back_recv.at[half], back_recv.at[half], back_sems.at[1, half]).wait()
         for duo in range(repeat // 2):
@@ -367,6 +371,13 @@
                         convolved + skip_ref[:, lanes] * mixed
                     )
                     out_ref[:, lanes] = gated.astype(bf16)
+                    store = pltpu.make_async_copy(
+                        out_ref.at[:, lanes],
+                        out_hbm.at[:, lanes],
+                        store_sems.at[len(stores)],
+                    )
+                    store.start()
+                    stores.append(store)
 
     loads[3].wait()
     loads[4].wait()
@@ -380,6 +391,8 @@
         pltpu.make_async_copy(others, others, send_sems.at[0, half]).wait()
         others = back_send.at[half, pl.ds(0, devices - 1)]
         pltpu.make_async_copy(others, others, back_sems.at[0, half]).wait()
+    for store in stores:
+        store.wait()
 
 
 def fused(gate_outer, gate_inner, values_in, filter_taps, skip_gain):
@@ -398,8 +411,9 @@
         functools.partial(conv_kernel, seq_count, ch_count, repeat),
         out_shape=jax.ShapeDtypeStruct((length_dev, width), bf16),
         in_specs=[pl.BlockSpec(memory_space=pltpu.HBM)] * 5,
-        out_specs=pl.BlockSpec(memory_space=pltpu.VMEM),
+        out_specs=pl.BlockSpec(memory_space=pltpu.HBM),
         scratch_shapes=[
+            pltpu.VMEM((length_dev, width), bf16),
             pltpu.VMEM((length_dev, width), bf16),
             pltpu.VMEM((length_dev, width), bf16),
             pltpu.VMEM((length_dev, width), bf16),
@@ -421,9 +435,10 @@
             pltpu.SemaphoreType.DMA((2,)),
             pltpu.SemaphoreType.DMA((2, 2)),
             pltpu.SemaphoreType.DMA((2, 2)),
+            pltpu.SemaphoreType.DMA((width // LANES,)),
         ],
         compiler_params=pltpu.CompilerParams(
-            collective_id=0, has_side_effects=True, vmem_limit_bytes=40 * 1024 * 1024
+            collective_id=0, has_side_effects=True, vmem_limit_bytes=64 * 1024 * 1024
         ),
     )(gate_outer, gate_inner, values_in, filter_taps, skip_gain[None, :])
 

time: 40.2 us -> 36.8 us (0.915)
  local copies, waits for them, and re-layouts: 5.45 us -> 1.88 us
    unnamed x11 -> x1, local copies, waits for them, and re-layouts: 5.45 us -> 1.88 us
    pallas_call x1, Pallas kernels: 34.4 us -> 34.8 us  [fused(): pl.pallas_call(functools.partial(conv_kernel, seq_count, ch_count, repeat...]
where the time goes in v3:
time: 36.8 us; the launch traced here: 36.7 us
  Pallas kernels  34.8 us (95%)
  local copies, waits for them, and re-layouts  1.88 us (5%)
    pallas_call x1, Pallas kernels, fused(): pl.pallas_call(functools.partial(conv_kernel, seq_count, ch_count, repeat...  34.8 us
    unnamed x1, local copies, waits for them, and re-layouts  1.88 us

profile of v3, /device:TPU:0, one launch (start us, length us, event | category | flops | bytes accessed | tf_op | source)
XLA Modules:
  0.0 36.7 jit_solution(9410841798432848019)
XLA Ops:
  0.0 34.8 %shard_map.55 = bf16[128,2048]{1,0:T(8,128)(2,1)} custom-call(bf16[128,2048]{1,0:T(8,128)(2,1)} %outer_hbm.1, bf16[128,2048]{1,0:T(8,128)(2,1)} %inner_hbm.1, bf16[128,2048]{1,0:T(8,128)(2,1)} %values_hbm.1, bf16[128,256]{1,0:T(8,128)(2,1)} %taps_hbm.1, f32[1,2048]{1,0:T(1,128)} %bitcast.1), custom_call_target="tpu_custom_call" | custom-call | tf_op jit(solution)/shard_map/pallas_call | solution.py:410
  34.8 1.9 %copy.7 = bf16[128,2048]{1,0:T(8,128)(2,1)} copy(bf16[128,2048]{1,0:T(8,128)(2,1)} %shard_map.55) | data formatting | bytes 1048576

commit v4 on v3

--- a/solution.py
+++ b/solution.py
@@ -202,8 +202,7 @@
         load.start()
 
     def partner(step):
-        offset = devices // 2 + step // 2 * (2 * (step % 2) - 1)
-        flat = lax.rem(me + offset, devices)
+        flat = lax.rem(me + step, devices)
         return flat // ch_count, lax.rem(flat, ch_count)
 
     barrier = pltpu.get_barrier_semaphore()

time: 36.8 us -> 35.4 us (0.962)
  Pallas kernels: 34.8 us -> 33.3 us
    pallas_call x1, Pallas kernels: 34.8 us -> 33.3 us  [fused(): pl.pallas_call(functools.partial(conv_kernel, seq_count, ch_count, repeat...]
where the time goes in v4:
time: 35.4 us; the launch traced here: 35.2 us
  Pallas kernels  33.3 us (94%)
  local copies, waits for them, and re-layouts  1.88 us (5%)
    pallas_call x1, Pallas kernels, fused(): pl.pallas_call(functools.partial(conv_kernel, seq_count, ch_count, repeat...  33.3 us
    unnamed x1, local copies, waits for them, and re-layouts  1.88 us

profile of v4, /device:TPU:0, one launch (start us, length us, event | category | flops | bytes accessed | tf_op | source)
XLA Modules:
  0.0 35.2 jit_solution(3718080009253335396)
XLA Ops:
  0.0 33.3 %shard_map.55 = bf16[128,2048]{1,0:T(8,128)(2,1)} custom-call(bf16[128,2048]{1,0:T(8,128)(2,1)} %outer_hbm.1, bf16[128,2048]{1,0:T(8,128)(2,1)} %inner_hbm.1, bf16[128,2048]{1,0:T(8,128)(2,1)} %values_hbm.1, bf16[128,256]{1,0:T(8,128)(2,1)} %taps_hbm.1, f32[1,2048]{1,0:T(1,128)} %bitcast.1), custom_call_target="tpu_custom_call" | custom-call | tf_op jit(solution)/shard_map/pallas_call | solution.py:409
  33.3 1.9 %copy.7 = bf16[128,2048]{1,0:T(8,128)(2,1)} copy(bf16[128,2048]{1,0:T(8,128)(2,1)} %shard_map.55) | data formatting | bytes 1048576

commit v5 on v4

--- a/solution.py
+++ b/solution.py
@@ -238,6 +238,7 @@
     loads[1].wait()
     loads[2].wait()
     mix(0)
+    mix(1)
 
     pl.semaphore_wait(barrier, devices - 1)
 
@@ -273,7 +274,6 @@
             ).start()
 
     send_out(0)
-    mix(1)
     send_out(1)
 
     group = 2 * members
@@ -285,22 +285,22 @@
     col = lax.broadcasted_iota(jnp.int32, (LANES, LANES), 1)
     upper = col >= row
 
-    @pl.loop(0, 2 * pairs)
-    def _(pair):
-        for side in range(2):
-            before = jnp.zeros((LANES, LANES), f32)
-            for lag in range(seq_count):
-                line = taps_wide[pl.ds(lag * 2 * HALF_ROWS + pair * 2 + side, 1), :]
-                spread = jnp.broadcast_to(line, (LANES, LANES))
-                rolled = pltpu.roll(spread, 0, 1, stride=1, stride_axis=0)
-                toeplitz_ref[
-                    pair, lag * LANES : (lag + 1) * LANES, side * LANES : (side + 1) * LANES
-                ] = jnp.where(upper, rolled, before).astype(bf16)
-                before = rolled
-
     block_rows = members * HALF_ROWS
 
     def convolve(half):
+        @pl.loop(half * pairs, (half + 1) * pairs)
+        def _(pair):
+            for side in range(2):
+                before = jnp.zeros((LANES, LANES), f32)
+                for lag in range(seq_count):
+                    line = taps_wide[pl.ds(lag * 2 * HALF_ROWS + pair * 2 + side, 1), :]
+                    spread = jnp.broadcast_to(line, (LANES, LANES))
+                    rolled = pltpu.roll(spread, 0, 1, stride=1, stride_axis=0)
+                    toeplitz_ref[
+                        pair, lag * LANES : (lag + 1) * LANES, side * LANES : (side + 1) * LANES
+                    ] = jnp.where(upper, rolled, before).astype(bf16)
+                    before = rolled
+
         pltpu.make_async_copy(recv_ref.at[half], recv_ref.at[half], send_sems.at[1, half]).wait()
         recv_wide[...] = recv_ref[half].reshape(recv_wide.shape).astype(f32)
 

time: 35.4 us -> 35.4 us (level)
  no operation moved by 1% of the time
where the time goes in v5:
time: 35.4 us; the launch traced here: 35.2 us
  Pallas kernels  33.3 us (94%)
  local copies, waits for them, and re-layouts  1.88 us (5%)
    pallas_call x1, Pallas kernels, fused(): pl.pallas_call(functools.partial(conv_kernel, seq_count, ch_count, repeat...  33.3 us
    unnamed x1, local copies, waits for them, and re-layouts  1.88 us

profile of v5, /device:TPU:0, one launch (start us, length us, event | category | flops | bytes accessed | tf_op | source)
XLA Modules:
  0.0 35.2 jit_solution(7568318629332618733)
XLA Ops:
  0.0 33.3 %shard_map.55 = bf16[128,2048]{1,0:T(8,128)(2,1)} custom-call(bf16[128,2048]{1,0:T(8,128)(2,1)} %outer_hbm.1, bf16[128,2048]{1,0:T(8,128)(2,1)} %inner_hbm.1, bf16[128,2048]{1,0:T(8,128)(2,1)} %values_hbm.1, bf16[128,256]{1,0:T(8,128)(2,1)} %taps_hbm.1, f32[1,2048]{1,0:T(1,128)} %bitcast.1), custom_call_target="tpu_custom_call" | custom-call | tf_op jit(solution)/shard_map/pallas_call | solution.py:409
  33.3 1.9 %copy.7 = bf16[128,2048]{1,0:T(8,128)(2,1)} copy(bf16[128,2048]{1,0:T(8,128)(2,1)} %shard_map.55) | data formatting | bytes 1048576
